TPU v7x, 256 devices: a whole 4x4x8 slice. The times are simulated.
256 devices in a mesh: dp: 16 (over y, x_lo, core), tensor: 16 (over z, x_hi).
Axes of the slice: x: 4 (x_hi: 2, x_lo: 2; x = x_hi * 2 + x_lo), y: 4, z: 8, core: 2. Of those that a mesh axis runs over, the one named last changes fastest.
Arguments:
- inputs: bfloat16 [2048, 4096], P('dp', 'tensor'), may hold values from -6 to 6
- gate_blocks: bfloat16 [16, 112, 128, 128], P('dp', 'tensor'), may hold values from -0.125 to 0.125
- up_blocks: bfloat16 [16, 112, 128, 128], P('dp', 'tensor'), may hold values from -0.125 to 0.125
- block_mask: int32 [32, 112], P(None, 'tensor'), may hold values from 0 to 1, as said below
- grad_hidden: bfloat16 [2048, 14336], P('dp', 'tensor'), may hold values from -6 to 6
Outputs:
- hidden: bfloat16 [2048, 14336], P('dp', 'tensor')
- grad_inputs: bfloat16 [2048, 4096], P('dp', 'tensor')
- grad_gate_blocks: bfloat16 [16, 112, 128, 128], P('dp', 'tensor')
- grad_up_blocks: bfloat16 [16, 112, 128, 128], P('dp', 'tensor')
Inputs may be any that keep to these rules, and one draw needn't show every extreme that they name: Every column of block_mask holds exactly 16 ones; the number of ones in a row differs from row to row and may be anything from 0 to 112.
All inputs are finite; a program needn't handle non-finite values.
Results may differ from a plain program's by a relative error of at most 0.023.
Values may be sent and summed in bfloat16 or wider, within the bound.
A program may use at most 128 MiB of HBM per device.

v0:
```python
import math

import jax
import jax.numpy as jnp
from jax import lax
from jax.sharding import PartitionSpec as P


def tables(block_mask, keep_total):
    row_rank = jnp.cumsum(block_mask, axis=0) - 1
    levels = jnp.arange(keep_total, dtype=jnp.int32)
    chosen = (block_mask[None] == 1) & (row_rank[None] == levels[:, None, None])
    row_ids = jnp.arange(block_mask.shape[0], dtype=jnp.int32)
    row_index = jnp.sum(jnp.where(chosen, row_ids[None, :, None], 0), axis=1)
    selector = jnp.transpose(chosen, (0, 2, 1)).astype(jnp.float32)
    return (row_index, selector)


def per_device(inputs, gate_blocks, up_blocks, block_mask, grad_hidden):
    tok_rows = inputs.shape[0]
    keep_total = gate_blocks.shape[0] * lax.axis_size("dp")
    col_local = gate_blocks.shape[1]
    side = gate_blocks.shape[2]
    row_index, selector = tables(block_mask, keep_total)
    whole = lax.all_gather(inputs, "tensor", axis=1, tiled=True)
    row_blocks = whole.shape[1] // side
    blocks = whole.reshape(tok_rows, row_blocks, side)
    pieces = (
        lax.all_gather(gate_blocks, "dp", axis=0, tiled=True),
        lax.all_gather(up_blocks, "dp", axis=0, tiled=True),
    )
    rows_here = row_index
    taken = jnp.take(blocks, rows_here, axis=1)
    gate_acc = jnp.einsum("tkcj,kcjh->tch", taken, pieces[0], preferred_element_type=jnp.float32)
    up_acc = jnp.einsum("tkcj,kcjh->tch", taken, pieces[1], preferred_element_type=jnp.float32)
    sig_gate = jax.nn.sigmoid(gate_acc)
    hidden = (gate_acc * sig_gate * up_acc).astype(jnp.bfloat16)
    upstream = grad_hidden.reshape(tok_rows, col_local, side).astype(jnp.float32)
    d_gate = (upstream * up_acc * sig_gate * (1.0 + gate_acc * (1.0 - sig_gate))).astype(
        jnp.bfloat16
    )
    d_up = (upstream * gate_acc * sig_gate).astype(jnp.bfloat16)
    pieces = (
        lax.all_gather(gate_blocks, "dp", axis=0, tiled=True),
        lax.all_gather(up_blocks, "dp", axis=0, tiled=True),
    )
    contrib = jnp.einsum("tch,kcjh->tkcj", d_gate, pieces[0], preferred_element_type=jnp.float32)
    grad_acc = jnp.einsum(
        "tkcj,kcr->trj",
        contrib + jnp.einsum("tch,kcjh->tkcj", d_up, pieces[1], preferred_element_type=jnp.float32),
        selector,
    )
    grad_inputs = lax.psum_scatter(
        grad_acc.reshape(tok_rows, row_blocks * side).astype(jnp.bfloat16),
        "tensor",
        scatter_dimension=1,
        tiled=True,
    )
    grad_scale = 1.0 / math.sqrt(tok_rows * lax.axis_size("dp"))
    rows_here = row_index
    taken = jnp.take(blocks, rows_here, axis=1)
    gate_term = jnp.einsum("tkcj,tch->kcjh", taken, d_gate, preferred_element_type=jnp.float32)
    up_term = jnp.einsum("tkcj,tch->kcjh", taken, d_up, preferred_element_type=jnp.float32)
    summed = lax.psum_scatter(
        (jnp.stack([gate_term, up_term], axis=1) * grad_scale).astype(jnp.bfloat16),
        "dp",
        scatter_dimension=0,
        tiled=True,
    ).astype(jnp.float32)
    grad_gate_blocks = summed[:, 0].astype(jnp.bfloat16)
    grad_up_blocks = summed[:, 1].astype(jnp.bfloat16)
    return (
        hidden.reshape(tok_rows, col_local * side),
        grad_inputs,
        grad_gate_blocks,
        grad_up_blocks,
    )


def solution(mesh):
    return jax.shard_map(
        per_device,
        mesh=mesh,
        in_specs=(
            P("dp", "tensor"),
            P("dp", "tensor", None, None),
            P("dp", "tensor", None, None),
            P(None, "tensor"),
            P("dp", "tensor"),
        ),
        out_specs=(
            P("dp", "tensor"),
            P("dp", "tensor"),
            P("dp", "tensor", None, None),
            P("dp", "tensor", None, None),
        ),
        check_vma=False,
    )
```

profile of v0, /device:TPU:2, one launch (start us, length us, event | category | flops | bytes accessed | tf_op | source)
XLA Modules:
  0.0 586.2 jit_solution(9665724028445907382)
XLA Ops:
  7.2 1.6 copy.71
  8.9 0.7 all-gather.8.cloned.1.call-update
  10.3 1.1 copy.77
  11.4 0.8 copy.68
  13.6 78.5 %all-gather.4.cloned.1.call-done = bf16[128,4096]{0,1:T(8,128)(2,1)} async-done(((bf16[128,256]{0,1:T(8,128)(2,1)}), bf16[128,4096]{0,1:T(8,128)(2,1)}) %all-gather.4.cloned.1.call-update) | async-done | bytes 1048592 | tf_op jit(solution)/shard_map/all_gather | solution.py:25
  92.1 1.6 copy.73
  93.7 2.9 gather_fusion
  96.6 33.5 %all-gather.8.cloned.1.call-done = bf16[16,7,128,128]{3,2,1,0:T(8,128)(2,1)} async-done(((bf16[1,7,128,128]{3,2,1,0:T(8,128)(2,1)}), bf16[16,7,128,128]{3,2,1,0:T(8,128)(2,1)}) %all-gather.8.cloned.1.call-update) | async-done | bytes 3670032 | tf_op jit(solution)/shard_map/all_gather | solution.py:30
  130.1 4.6 convolution_bitcast_fusion
  134.7 36.6 %all-gather.6.cloned.1.call-done = bf16[16,7,128,128]{3,2,1,0:T(8,128)(2,1)} async-done(((bf16[1,7,128,128]{3,2,1,0:T(8,128)(2,1)}), bf16[16,7,128,128]{3,2,1,0:T(8,128)(2,1)}) %all-gather.6.cloned.1.call-update) | async-done | bytes 3670032 | tf_op jit(solution)/shard_map/all_gather | solution.py:29
  171.3 4.9 multiply_convert_fusion.1
  176.2 4.2 fusion.14
  180.4 4.1 fusion.11
  184.6 10.2 %fusion = bf16[16,2,7,128,128]{3,4,0,2,1:T(8,128)(2,1)} fusion(f32[16,1,7,128,128]{3,4,0,2,1:T(8,128)} %fusion.14, f32[16,1,7,128,128]{3,4,0,2,1:T(8,128)} %fusion.11), kind=kLoop, calls=%fused_computation.2 | loop fusion | flops 11010048 | bytes 22020096 | tf_op jit(solution)/shard_map/convert_element_type | solution.py:65
  195.5 3.3 fusion.3
  198.8 1.2 add_bitcast_fusion
  200.0 2.4 bitcast_convert_fusion
  202.4 1.4 copy.121
  204.4 0.8 copy.85
  205.3 165.0 %all-reduce.3.cloned.1.call-done = bf16[16,2,7,128,128]{3,4,0,2,1:T(8,128)(2,1)} async-done(((bf16[16,2,7,128,128]{3,4,0,2,1:T(8,128)(2,1)}), bf16[16,2,7,128,128]{3,4,0,2,1:T(8,128)(2,1)}) %all-reduce.3.cloned.1.call-update) | async-done | bytes 7340048
  370.2 1.7 dynamic-slice_bitcast_fusion
  372.0 0.8 copy.86
  372.8 0.8 copy.87
  373.6 206.0 %reduce-scatter.5.cloned.1.call-done = bf16[128,256]{1,0:T(8,128)(2,1)} async-done(((bf16[128,4096]{1,0:T(8,128)(2,1)}), bf16[128,256]{1,0:T(8,128)(2,1)}) %reduce-scatter.5.cloned.1.call-update) | async-done | bytes 65552 | tf_op jit(solution)/shard_map/reduce_scatter | solution.py:53
  (31 shorter events, 3.5 us)
Async XLA Ops:
  7.2 84.9 %all-gather.4.cloned.1.call-start = ((), (), s32[]{:S(2)}) async-start(), calls=%async_computation.1 | async-start | bytes 1114112 | tf_op jit(solution)/shard_map/all_gather | solution.py:25
  8.8 121.3 %all-gather.8.cloned.1.call-start = ((), (), s32[]{:S(2)}) async-start(), calls=%async_computation.3 | async-start | bytes 3899392 | tf_op jit(solution)/shard_map/all_gather | solution.py:30
  9.6 161.8 %all-gather.6.cloned.1.call-start = ((), (), s32[]{:S(2)}) async-start(), calls=%async_computation.2 | async-start | bytes 3899392 | tf_op jit(solution)/shard_map/all_gather | solution.py:29
  10.3 359.9 %all-reduce.3.cloned.1.call-start = ((), (), s32[]{:S(2)}) async-start(), calls=%async_computation.5 | async-start | bytes 14680064
  171.3 4.9 copy-start
  194.8 0.7 copy-start.2
  194.8 384.8 %reduce-scatter.5.cloned.1.call-start = ((), (), s32[]{:S(2)}) async-start(), calls=%async_computation.4 | async-start | bytes 1114112 | tf_op jit(solution)/shard_map/reduce_scatter | solution.py:53
  195.5 3.4 copy-start.1
  200.0 3.8 copy-start.3
Sparse Core Ops, SparseCore 0:
  11.2 80.8 all-gather.3
  93.9 36.1 all-gather.7
  132.0 39.3 all-gather.5
  194.9 175.2 all-reduce.2
  374.5 205.0 reduce-scatter.4
where the time goes:
time: 587 us; the launch traced here: 586 us
  waiting for transfers between devices  521 us (89%)
  matrix products  24.7 us (4%)
  local copies, waits for them, and re-layouts  14.9 us (3%)
  between operations  13.9 us (2%)
  other arithmetic  11.2 us (2%)
    reduce_scatter x1, waiting for transfers between devices, per_device(): lax.psum_scatter(grad_acc.reshape(tok_rows, row_blocks * side).astype(jnp...  206 us
    unnamed x6, waiting for transfers between devices  166 us
    all_gather x1, waiting for transfers between devices, per_device(): whole = lax.all_gather(inputs, 'tensor', axis=1, tiled=True)  78.5 us
    all_gather x1, waiting for transfers between devices, per_device(): lax.all_gather(gate_blocks, 'dp', axis=0, tiled=True)  36.6 us
    all_gather x1, waiting for transfers between devices, per_device(): lax.all_gather(up_blocks, 'dp', axis=0, tiled=True)  33.5 us
  transfers between devices with their start and end apart: 5, of which 5 were waited for; matrix products, arithmetic and copies ran while one was open for 4% of the time, Pallas kernels for 0%

commit v1 on v0

v1 whole, which is shorter than its diff:
```python
import jax
import jax.numpy as jnp
from jax import lax
from jax.experimental import pallas as pl
from jax.experimental.pallas import tpu as pltpu
from jax.sharding import PartitionSpec as P

MESH = pl.DeviceIdType.MESH
F32, BF16 = jnp.float32, jnp.bfloat16
B = 128
NC = 7
KEEP = 16
RB = 32
SCALE = 2048.0**-0.5


def kernel(
    x_ref, g_ref, u_ref, mask_ref, gh_ref,
    hid_ref, dx_ref, gg_ref, gu_ref,
    wbuf, xbuf, xt, dt, part_out, part_in, part, leave, land, up_s, up_r, dn_s, dn_r, last_s, last_r,
    rank, rows, following,
    ag_s, ag_r, in_s, in_r, rs_s, rs_r, dx_ss, dx_rs,
):
    dp, tn = lax.axis_index("dp"), lax.axis_index("tensor")
    y, x, k = dp // 4, (dp // 2) % 2, dp % 2
    z, h = tn // 2, tn % 2
    yp, ym, y2 = (y + 1) % 4, (y + 3) % 4, (y + 2) % 4
    zp, zm = (z + 1) % 8, (z + 7) % 8
    xo, ko, ho = 1 - x, 1 - k, 1 - h

    def slot(yy, xx, kk):
        return yy * 4 + xx * 2 + kk

    to_sib = (slot(y, x, ko), tn)
    to_x = (slot(y, xo, k), tn)
    to_yp = (slot(yp, x, k), tn)
    to_ym = (slot(ym, x, k), tn)
    to_zp = (dp, zp * 2 + h)
    to_zm = (dp, zm * 2 + h)
    to_h = (dp, z * 2 + ho)
    neighbours = (to_sib, to_x, to_yp, to_ym, to_zp, to_zm, to_h)

    barrier = pltpu.get_barrier_semaphore()
    for there in neighbours:
        pl.semaphore_signal(barrier, inc=1, device_id=there, device_id_type=MESH)

    for c in range(NC):
        wbuf[dp, c, 0] = g_ref[0, c]
        wbuf[dp, c, 1] = u_ref[0, c]
        wbuf[KEEP, c] = jnp.zeros((2, B, B), BF16)
    for b in range(2):
        xbuf[tn * 2 + b] = x_ref[:, b * B : (b + 1) * B]
    pl.semaphore_wait(barrier, len(neighbours))

    ring = ((y, x), (y, xo), (ym, x), (yp, x), (ym, xo), (yp, xo), (y2, x), (y2, xo))
    OWN, N, PP, MM, NP, NM, P2, M2 = range(8)

    def ag(kind, which, c, there, core):
        s = slot(*ring[which], core)
        return pltpu.make_async_remote_copy(
            src_ref=wbuf.at[s, c], dst_ref=wbuf.at[s, c],
            send_sem=ag_s.at[kind, c], recv_sem=ag_r.at[kind, c],
            device_id=there, device_id_type=MESH,
        )

    def ag_send(kind, which, c, there):
        ag(kind, which, c, there, k).start()

    def ag_got(kind, c):
        ag(kind, kind, c, to_x, k).wait_recv()

    def ag_share(which, c):
        ag(8 + which, which, c, to_sib, k).start()

    def ag_own(c):
        ag_send(N, OWN, c, to_x)
        ag_send(PP, OWN, c, to_yp)
        ag_send(MM, OWN, c, to_ym)
        ag_share(OWN, c)

    def ag_second(c):
        ag_got(N, c)
        ag_send(NP, N, c, to_yp)
        ag_send(NM, N, c, to_ym)
        ag_share(N, c)

    def ag_third(c):
        ag_got(PP, c)
        ag_send(P2, PP, c, to_yp)
        ag_share(PP, c)
        ag_got(MM, c)
        ag_share(MM, c)
        ag_got(NM, c)
        ag_send(M2, NM, c, to_ym)
        ag_share(NM, c)
        ag_got(NP, c)
        ag_share(NP, c)

    def ag_fourth(c):
        ag_got(P2, c)
        ag_share(P2, c)
        ag_got(M2, c)
        ag_share(M2, c)

    def ag_end(c):
        for which in range(8):
            ag(8 + which, which, c, to_sib, ko).wait_recv()

    def inp(sem, zz, hh, there):
        at = pl.ds(((zz + 8) % 8) * 4 + hh * 2, 2)
        return pltpu.make_async_remote_copy(
            src_ref=xbuf.at[at], dst_ref=xbuf.at[at],
            send_sem=in_s.at[sem], recv_sem=in_r.at[sem],
            device_id=there, device_id_type=MESH,
        )

    own_up, oth_dn, own_dn, oth_up = 0, 4, 8, 11

    inp(0, z, h, to_h).start()
    inp(own_up + 1, z, h, to_zp).start()
    inp(own_dn + 1, z, h, to_zm).start()
    for c in range(NC):
        ag_own(c)

    def column_tables(c, _):
        def count(r, seen):
            here = mask_ref[r, c]
            rank[r, c] = jnp.where(here == 1, jnp.minimum(seen, KEEP - 1), KEEP)
            return seen + here

        lax.fori_loop(0, RB, count, jnp.int32(0))

        def back(q, after):
            r = RB - 1 - q
            after = jnp.where(mask_ref[r, c] == 1, r, after)
            following[r] = after
            return after

        lax.fori_loop(0, RB, back, jnp.int32(RB - 1))

        def pick(kk, r):
            r = following[jnp.minimum(r, RB - 1)]
            rows[kk, c] = r
            return r + 1

        lax.fori_loop(0, KEEP, pick, jnp.int32(0))
        return 0

    lax.fori_loop(0, NC, column_tables, 0)

    inp(0, z, ho, to_h).wait_recv()
    inp(oth_up + 1, z, ho, to_zp).start()
    inp(oth_dn + 1, z, ho, to_zm).start()
    for j in (1, 2, 3, 4):
        inp(own_up + j, z - j, h, to_zp).wait_recv()
        if j < 4:
            inp(own_up + j + 1, z - j, h, to_zp).start()
        if j < 4:
            inp(own_dn + j, z + j, h, to_zm).wait_recv()
            if j < 3:
                inp(own_dn + j + 1, z + j, h, to_zm).start()
            inp(oth_up + j, z - j, ho, to_zp).wait_recv()
            if j < 3:
                inp(oth_up + j + 1, z - j, ho, to_zp).start()
        inp(oth_dn + j, z + j, ho, to_zm).wait_recv()
        if j < 4:
            inp(oth_dn + j + 1, z + j, ho, to_zm).start()
        for c in ((), (0, 1), (2, 3), (4, 5, 6), ())[j]:
            ag_second(c)
        for c in ((), (), (0,), (1,), ())[j]:
            ag_third(c)

    def turn(r, _):
        xt[r] = xbuf[r].T
        return 0

    lax.fori_loop(0, RB, turn, 0)
    ag_fourth(0)

    A_UP, A_DN, C_UP, C_DN, E_UP, F_DN, G_X = range(7)

    goal = ((y2, x), (y2, xo), (yp, xo), (ym, x), (yp, x), (ym, xo), (y, xo), (y, x))
    MINE = 7

    def rs(kind, c, there):
        return pltpu.make_async_remote_copy(
            src_ref=leave.at[kind, c], dst_ref=land.at[kind, c],
            send_sem=rs_s.at[kind, c], recv_sem=rs_r.at[kind, c],
            device_id=there, device_id_type=MESH,
        )

    def rs_pair(c):
        return pltpu.make_async_remote_copy(
            src_ref=part_out.at[c], dst_ref=part_in.at[c],
            send_sem=rs_s.at[7, c], recv_sem=rs_r.at[7, c],
            device_id=to_sib, device_id_type=MESH,
        )

    def rs_got(kind, c):
        rs(kind, c, to_x).wait_recv()

    def total(c, goes, kinds):
        value = part[c, goes].astype(F32) + part_in[c, goes].astype(F32)
        for kind in kinds:
            value = value + land[kind, c].astype(F32)
        return value

    def rs_send(kind, c, there, kinds=()):
        leave[kind, c] = total(c, kind, kinds).astype(BF16)
        rs(kind, c, there).start()

    def rs_first(c):
        rs_pair(c).wait_recv()
        rs_send(A_UP, c, to_yp)
        rs_send(A_DN, c, to_ym)
        rs_send(C_UP, c, to_yp)
        rs_send(C_DN, c, to_ym)

    def rs_second(c):
        rs_got(A_UP, c)
        rs_send(E_UP, c, to_yp, (A_UP,))
        rs_got(A_DN, c)
        rs_send(F_DN, c, to_ym, (A_DN,))

    def rs_third(c):
        rs_got(C_UP, c)
        rs_got(F_DN, c)
        rs_send(G_X, c, to_x, (C_UP, F_DN))

    def rs_last(c):
        for kind in (C_DN, E_UP, G_X):
            rs_got(kind, c)
        value = total(c, MINE, (C_DN, E_UP, G_X)).astype(BF16)
        gg_ref[0, c] = value[0]
        gu_ref[0, c] = value[1]

    def weight(s, c):
        return jnp.concatenate([wbuf[s, c, 0], wbuf[s, c, 1]], axis=1)

    def compute(c):
        acc = jnp.zeros((B, 2 * B), F32)
        for s in range(0, KEEP, 2):
            lhs = jnp.concatenate([xbuf[rows[s, c]], xbuf[rows[s + 1, c]]], axis=1)
            rhs = jnp.concatenate([weight(s, c), weight(s + 1, c)], axis=0)
            acc = acc + jnp.dot(lhs, rhs, preferred_element_type=F32)
        gate, up = acc[:, :B], acc[:, B:]
        sig = jax.nn.sigmoid(gate)
        silu = gate * sig
        lanes = pl.ds(pl.multiple_of(c * B, B), B)
        hid_ref[:, lanes] = (silu * up).astype(BF16)
        grad = gh_ref[:, lanes].astype(F32)
        d_gate = (grad * up * sig * (1.0 + gate * (1.0 - sig))).astype(BF16)
        d_up = (grad * silu).astype(BF16)
        dt[c, :B] = d_gate.T
        dt[c, B:] = d_up.T
        delta = jnp.concatenate([d_gate, d_up], axis=1)
        for core, target in ((ko, part_out), (k, part)):
            for i in range(0, 8, 2):
                blocks = [xt[rows[slot(*goal[i + half], core), c]] for half in range(2)]
                lhs = jnp.concatenate(blocks, axis=0)
                out = (jnp.dot(lhs, delta, preferred_element_type=F32) * SCALE).astype(BF16)
                for half in range(2):
                    target[c, i + half, 0] = out[half * B : (half + 1) * B, :B]
                    target[c, i + half, 1] = out[half * B : (half + 1) * B, B:]
            if target is part_out:
                rs_pair(c).start()

    def column(c, _):
        @pl.when(c + 2 < NC)
        def _():
            ag_third(c + 2)

        @pl.when(c + 1 < NC)
        def _():
            ag_fourth(c + 1)

        ag_end(c)
        compute(c)

        @pl.when(c >= 1)
        def _():
            rs_first(c - 1)

        @pl.when(c >= 2)
        def _():
            rs_second(c - 2)

        @pl.when(c >= 3)
        def _():
            rs_third(c - 3)

        @pl.when(c >= 4)
        def _():
            rs_last(c - 4)

        return 0

    lax.fori_loop(0, NC, column, 0)

    def unit(zz):
        def one(c, acc):
            lhs = jnp.concatenate([weight(rank[zz * 4 + b, c], c) for b in range(4)], axis=0)
            return acc + jnp.dot(lhs, dt[c], preferred_element_type=F32)

        return lax.fori_loop(0, NC, one, jnp.zeros((4 * B, B), F32)).reshape(4, B, B)

    def ring_copy(src, dst, sem, there):
        return pltpu.make_async_remote_copy(
            src_ref=src, dst_ref=dst, send_sem=dx_ss.at[sem], recv_sem=dx_rs.at[sem],
            device_id=there, device_id_type=MESH,
        )

    def go_up(n):
        cut = pl.ds(0, 2 if n == 0 else 4)
        return ring_copy(up_s.at[n, cut], up_r.at[n, cut], n, to_zp)

    def go_down(n):
        cut = pl.ds(2, 2) if n == 0 else pl.ds(0, 4)
        return ring_copy(dn_s.at[n, cut], dn_r.at[n, cut], 4 + n, to_zm)

    far = unit((z + 4) % 8).astype(BF16)
    up_s[0, :2] = far[:2]
    go_up(0).start()
    dn_s[0, 2:] = far[2:]
    go_down(0).start()

    def step(n):
        mine = unit((z + 4 - n) % 8)
        go_up(n - 1).wait_recv()
        if n == 1:
            up_s[n, :2] = (mine[:2] + up_r[0, :2].astype(F32)).astype(BF16)
            up_s[n, 2:] = mine[2:].astype(BF16)
        else:
            up_s[n] = (mine + up_r[n - 1].astype(F32)).astype(BF16)
        go_up(n).start()
        mine = unit((z + 4 + n) % 8)
        go_down(n - 1).wait_recv()
        if n == 1:
            dn_s[n, :2] = mine[:2].astype(BF16)
            dn_s[n, 2:] = (mine[2:] + dn_r[0, 2:].astype(F32)).astype(BF16)
        else:
            dn_s[n] = (mine + dn_r[n - 1].astype(F32)).astype(BF16)
        go_down(n).start()

    rs_first(NC - 1)
    rs_second(NC - 2)
    rs_third(NC - 3)
    rs_last(NC - 4)
    step(1)
    rs_second(NC - 1)
    rs_third(NC - 2)
    rs_last(NC - 3)
    step(2)
    rs_third(NC - 1)
    rs_last(NC - 2)
    step(3)
    mine = unit(z)
    go_up(3).wait_recv()
    go_down(3).wait_recv()
    last_s[...] = (mine + up_r[3].astype(F32) + dn_r[3].astype(F32)).astype(BF16)
    across = ring_copy(last_s.at[pl.ds(ho * 2, 2)], last_r, 8, to_h)
    across.start()
    rs_last(NC - 1)
    across.wait_recv()
    for b in range(2):
        value = last_s[h * 2 + b].astype(F32) + last_r[b].astype(F32)
        dx_ref[:, b * B : (b + 1) * B] = value.T.astype(BF16)

    def sent(c, _):
        for kind in range(1, 16):
            ag(kind, 0, c, to_x, k).wait_send()
        for kind in range(7):
            rs(kind, c, to_x).wait_send()
        rs_pair(c).wait_send()
        return 0

    lax.fori_loop(0, NC, sent, 0)
    for sem in range(15):
        inp(sem, z, h, to_h).wait_send()
    for n in range(4):
        go_up(n).wait_send()
        go_down(n).wait_send()
    across.wait_send()


def per_device(inputs, gate_blocks, up_blocks, block_mask, grad_hidden):
    vmem = pl.BlockSpec(memory_space=pltpu.VMEM)
    dma = pltpu.SemaphoreType.DMA
    unit = (4, B, B)
    return pl.pallas_call(
        kernel,
        out_shape=(
            jax.ShapeDtypeStruct(grad_hidden.shape, BF16),
            jax.ShapeDtypeStruct(inputs.shape, BF16),
            jax.ShapeDtypeStruct(gate_blocks.shape, BF16),
            jax.ShapeDtypeStruct(up_blocks.shape, BF16),
        ),
        in_specs=[vmem, vmem, vmem, pl.BlockSpec(memory_space=pltpu.SMEM), vmem],
        out_specs=(vmem, vmem, vmem, vmem),
        scratch_shapes=[
            pltpu.VMEM((KEEP + 1, NC, 2, B, B), BF16),
            pltpu.VMEM((RB, B, B), BF16),
            pltpu.VMEM((RB, B, B), BF16),
            pltpu.VMEM((NC, 2 * B, B), BF16),
            pltpu.VMEM((NC, 8, 2, B, B), BF16),
            pltpu.VMEM((NC, 8, 2, B, B), BF16),
            pltpu.VMEM((NC, 8, 2, B, B), BF16),
            pltpu.VMEM((7, NC, 2, B, B), BF16),
            pltpu.VMEM((7, NC, 2, B, B), BF16),
            pltpu.VMEM((4,) + unit, BF16),
            pltpu.VMEM((4,) + unit, BF16),
            pltpu.VMEM((4,) + unit, BF16),
            pltpu.VMEM((4,) + unit, BF16),
            pltpu.VMEM(unit, BF16),
            pltpu.VMEM((2, B, B), BF16),
            pltpu.SMEM((RB, NC), jnp.int32),
            pltpu.SMEM((KEEP, NC), jnp.int32),
            pltpu.SMEM((RB,), jnp.int32),
            dma((16, NC)),
            dma((16, NC)),
            dma((15,)),
            dma((15,)),
            dma((8, NC)),
            dma((8, NC)),
            dma((9,)),
            dma((9,)),
        ],
        compiler_params=pltpu.CompilerParams(
            collective_id=0, has_side_effects=True, vmem_limit_bytes=56 * 2**20
        ),
        cost_estimate=pl.CostEstimate(
            flops=4 * 10**9, bytes_accessed=3 * 2**20, transcendentals=128 * 896
        ),
    )(inputs, gate_blocks, up_blocks, block_mask, grad_hidden)


def solution(mesh):
    return jax.shard_map(
        per_device,
        mesh=mesh,
        in_specs=(
            P("dp", "tensor"),
            P("dp", "tensor", None, None),
            P("dp", "tensor", None, None),
            P(None, "tensor"),
            P("dp", "tensor"),
        ),
        out_specs=(
            P("dp", "tensor"),
            P("dp", "tensor"),
            P("dp", "tensor", None, None),
            P("dp", "tensor", None, None),
        ),
        check_vma=False,
    )
```

time: 587 us -> 98.3 us (0.17)
  waiting for transfers between devices: 521 us -> 0 us
  Pallas kernels: 0 us -> 91.5 us
  matrix products: 24.7 us -> 0 us
  between operations: 13.9 us -> 0.66 us
  other arithmetic: 11.2 us -> 0 us
  local copies, waits for them, and re-layouts: 14.9 us -> 5.41 us
    reduce_scatter x1 -> x0, waiting for transfers between devices: 206 us -> none  [per_device(): lax.psum_scatter(grad_acc.reshape(tok_rows, row_blocks * side).astype(jnp...]
    unnamed x6 -> x0, waiting for transfers between devices: 166 us -> none
    all_gather x3 -> x0, waiting for transfers between devices: 149 us -> none  [the longest x1 78.5 us: per_device(): whole = lax.all_gather(inputs, 'tensor', axis=1, tiled=True)]
    pallas_call x0 -> x1, Pallas kernels: none -> 91.5 us  [per_device(): pl.pallas_call(kernel, out_shape=(jax.ShapeDtypeStruct(grad_hidden.shape,...]
    dot_general x7 -> x0, matrix products: 24.7 us -> none  [the longest x1 4.88 us: per_device(): jnp.einsum('tkcj,kcjh->tch', taken, pieces[0], preferred_element_type=jnp...]
    convert_element_type x1 -> x0, other arithmetic: 10.2 us -> none  [per_device(): (jnp.stack([gate_term, up_term], axis=1) * grad_scale).astype(jnp.bfloat16)]
  transfers between devices with their start and end apart: 5 -> 0, of which waited for: 5 -> 0; matrix products, arithmetic and copies ran while one was open for 4% -> 0% of each run, Pallas kernels for 0% -> 0%
where the time goes in v1:
time: 98.3 us; the launch traced here: 97.6 us
  Pallas kernels  91.5 us (93%)
  local copies, waits for them, and re-layouts  5.41 us (6%)
    pallas_call x1, Pallas kernels, per_device(): pl.pallas_call(kernel, out_shape=(jax.ShapeDtypeStruct(grad_hidden.shape,...  91.5 us
    unnamed x11, local copies, waits for them, and re-layouts  5.41 us

profile of v1, /device:TPU:2, one launch (start us, length us, event | category | flops | bytes accessed | tf_op | source)
XLA Modules:
  0.0 97.6 jit_solution(18437944551103600578)
XLA Ops:
  0.6 1.4 %copy.9.mask_ref = s32[32,7]{1,0:T(8,128)} copy(s32[32,7]{0,1:T(8,128)} %param.8) | data formatting | bytes 1792 | tf_op args[3]
  2.0 91.5 %shard_map.84 = (bf16[128,896]{1,0:T(8,128)(2,1)}, bf16[128,256]{1,0:T(8,128)(2,1)}, bf16[1,7,128,128]{3,2,1,0:T(8,128)(2,1)}, bf16[1,7,128,128]{3,2,1,0:T(8,128)(2,1)}) custom-call(bf16[128,256]{1,0:T(8,128)(2,1)} %x_ref.1, bf16[1,7,128,128]{3,2,1,0:T(8,128)(2,1)} %g_ref.1, bf16[1,7,128,128]{3,2,1,0:T(8,128)(2,1)} %u_ref.1, s32[32,7]{1,0:T(8,128)} %copy.9.mask_ref, ...), custom_call_target="tpu_custom_call" | custom-call | flops 4000000000 | bytes 3145728 | tf_op jit(solution)/shard_map/pallas_call | solution.py:390
  93.5 0.0 copy-start.2
  93.5 0.0 copy-start.1
  93.6 1.7 %copy.14 = bf16[128,896]{1,0:T(8,128)(2,1)} copy(bf16[128,896]{1,0:T(8,128)(2,1)} %get-tuple-element.8) | data formatting | bytes 458752
  95.2 0.0 copy-done.2
  95.2 0.6 copy.15
  95.9 0.0 copy-done.1
  95.9 0.0 copy-start
  95.9 0.7 copy.16
  96.6 0.3 copy-done
  96.9 0.7 copy.17
Async XLA Ops:
  93.5 1.7 %copy-start.2 = (bf16[128,256]{1,0:T(8,128)(2,1)S(1)}, bf16[128,256]{1,0:T(8,128)(2,1)}, u32[]{:S(2)}) copy-start(bf16[128,256]{1,0:T(8,128)(2,1)} %get-tuple-element.9) | copy-start | bytes 196612
  93.5 2.3 %copy-start.1 = (bf16[1,7,128,128]{3,2,1,0:T(8,128)(2,1)S(1)}, bf16[1,7,128,128]{3,2,1,0:T(8,128)(2,1)}, u32[]{:S(2)}) copy-start(bf16[1,7,128,128]{3,2,1,0:T(8,128)(2,1)} %get-tuple-element.10) | copy-start | bytes 688132
  95.9 1.0 %copy-start = (bf16[1,7,128,128]{3,2,1,0:T(8,128)(2,1)S(1)}, bf16[1,7,128,128]{3,2,1,0:T(8,128)(2,1)}, u32[]{:S(2)}) copy-start(bf16[1,7,128,128]{3,2,1,0:T(8,128)(2,1)} %get-tuple-element.11) | copy-start | bytes 688132

commit v2 on v1

--- a/solution.py
+++ b/solution.py
@@ -102,6 +102,49 @@
         ag_got(M2, c)
         ag_share(M2, c)
 
+    HALF = 0
+
+    def ag_half(kind, which, c, half, there):
+        s = slot(*ring[which], k)
+        return pltpu.make_async_remote_copy(
+            src_ref=wbuf.at[s, c, half], dst_ref=wbuf.at[s, c, half],
+            send_sem=ag_s.at[kind, c], recv_sem=ag_r.at[kind, c],
+            device_id=there, device_id_type=MESH,
+        )
+
+    def ag_second_odd(c):
+        ag_got(PP, c)
+        ag_half(P2, PP, c, 0, to_yp).start()
+        ag_send(NP, PP, c, to_x)
+        ag_share(PP, c)
+        ag_got(MM, c)
+        ag_half(HALF, MM, c, 1, to_ym).start()
+        ag_send(NM, MM, c, to_x)
+        ag_share(MM, c)
+        ag_got(N, c)
+        ag_share(N, c)
+
+    def ag_third_odd(c):
+        ag_half(P2, P2, c, 0, to_yp).wait_recv()
+        ag_half(HALF, P2, c, 1, to_ym).wait_recv()
+        ag_send(M2, P2, c, to_x)
+        ag_share(P2, c)
+        ag_got(NP, c)
+        ag_share(NP, c)
+        ag_got(NM, c)
+        ag_share(NM, c)
+
+    def ag_fourth_odd(c):
+        ag_got(M2, c)
+        ag_share(M2, c)
+
+    def either(c, even, odd):
+        if isinstance(c, int):
+            (odd if c % 2 else even)(c)
+        else:
+            pl.when(c % 2 == 0)(lambda: even(c))
+            pl.when(c % 2 == 1)(lambda: odd(c))
+
     def ag_end(c):
         for which in range(8):
             ag(8 + which, which, c, to_sib, ko).wait_recv()
@@ -122,6 +165,10 @@
     for c in range(NC):
         ag_own(c)
 
+    inp(0, z, ho, to_h).wait_recv()
+    inp(oth_up + 1, z, ho, to_zp).start()
+    inp(oth_dn + 1, z, ho, to_zm).start()
+
     def column_tables(c, _):
         def count(r, seen):
             here = mask_ref[r, c]
@@ -148,9 +195,6 @@
 
     lax.fori_loop(0, NC, column_tables, 0)
 
-    inp(0, z, ho, to_h).wait_recv()
-    inp(oth_up + 1, z, ho, to_zp).start()
-    inp(oth_dn + 1, z, ho, to_zm).start()
     for j in (1, 2, 3, 4):
         inp(own_up + j, z - j, h, to_zp).wait_recv()
         if j < 4:
@@ -165,17 +209,20 @@
         inp(oth_dn + j, z + j, ho, to_zm).wait_recv()
         if j < 4:
             inp(oth_dn + j + 1, z + j, ho, to_zm).start()
-        for c in ((), (0, 1), (2, 3), (4, 5, 6), ())[j]:
-            ag_second(c)
-        for c in ((), (), (0,), (1,), ())[j]:
-            ag_third(c)
+        for c in ((), (0, 1, 2), (3, 4, 5, 6), (), ())[j]:
+            either(c, ag_second, ag_second_odd)
+        for c in ((), (), (0,), (1, 2, 3), (4, 5))[j]:
+            either(c, ag_third, ag_third_odd)
+        for c in ((), (), (), (0,), (1,))[j]:
+            either(c, ag_fourth, ag_fourth_odd)
 
     def turn(r, _):
         xt[r] = xbuf[r].T
         return 0
 
     lax.fori_loop(0, RB, turn, 0)
-    ag_fourth(0)
+    ag_third(6)
+    ag_fourth(2)
 
     A_UP, A_DN, C_UP, C_DN, E_UP, F_DN, G_X = range(7)
 
@@ -233,6 +280,55 @@
         value = total(c, MINE, (C_DN, E_UP, G_X)).astype(BF16)
         gg_ref[0, c] = value[0]
         gu_ref[0, c] = value[1]
+
+    X_Y2, X_YP, X_YM, X_Y, TO_UP, TO_DN, HALF_DN = 1, 2, 5, 6, 4, 3, 8
+
+    def rs_half(c, half):
+        there, sem = ((to_yp, 0), (to_ym, HALF_DN))[half]
+        return pltpu.make_async_remote_copy(
+            src_ref=leave.at[0, c, half], dst_ref=land.at[0, c, half],
+            send_sem=rs_s.at[sem, c], recv_sem=rs_r.at[sem, c],
+            device_id=there, device_id_type=MESH,
+        )
+
+    def rs_first_odd(c):
+        rs_pair(c).wait_recv()
+        for kind in (X_Y2, X_YP, X_YM, X_Y):
+            rs_send(kind, c, to_x)
+
+    def rs_second_odd(c):
+        rs_got(X_Y2, c)
+        leave[0, c] = total(c, 0, (X_Y2,)).astype(BF16)
+        rs_half(c, 0).start()
+        rs_half(c, 1).start()
+
+    def rs_third_odd(c):
+        for kind, came, half, there in ((TO_UP, X_YP, 0, to_yp), (TO_DN, X_YM, 1, to_ym)):
+            rs_got(came, c)
+            value = total(c, kind, (came,))
+            rs_half(c, half).wait_recv()
+            leave[kind, c, half] = (value[half] + land[0, c, half].astype(F32)).astype(BF16)
+            leave[kind, c, 1 - half] = value[1 - half].astype(BF16)
+            rs(kind, c, there).start()
+
+    def rs_last_odd(c):
+        for kind in (X_Y, TO_UP, TO_DN):
+            rs_got(kind, c)
+        value = total(c, MINE, (X_Y, TO_UP, TO_DN)).astype(BF16)
+        gg_ref[0, c] = value[0]
+        gu_ref[0, c] = value[1]
+
+    def rs_1(c):
+        either(c, rs_first, rs_first_odd)
+
+    def rs_2(c):
+        either(c, rs_second, rs_second_odd)
+
+    def rs_3(c):
+        either(c, rs_third, rs_third_odd)
+
+    def rs_4(c):
+        either(c, rs_last, rs_last_odd)
 
     def weight(s, c):
         return jnp.concatenate([wbuf[s, c, 0], wbuf[s, c, 1]], axis=1)
@@ -266,32 +362,24 @@
                 rs_pair(c).start()
 
     def column(c, _):
-        @pl.when(c + 2 < NC)
+        @pl.when(c + 3 < NC)
         def _():
-            ag_third(c + 2)
-
-        @pl.when(c + 1 < NC)
-        def _():
-            ag_fourth(c + 1)
+            either(c + 3, ag_fourth, ag_fourth_odd)
 
         ag_end(c)
         compute(c)
 
         @pl.when(c >= 1)
         def _():
-            rs_first(c - 1)
+            rs_1(c - 1)
 
         @pl.when(c >= 2)
         def _():
-            rs_second(c - 2)
+            rs_2(c - 2)
 
         @pl.when(c >= 3)
         def _():
-            rs_third(c - 3)
-
-        @pl.when(c >= 4)
-        def _():
-            rs_last(c - 4)
+            rs_3(c - 3)
 
         return 0
 
@@ -342,37 +430,52 @@
             dn_s[n] = (mine + dn_r[n - 1].astype(F32)).astype(BF16)
         go_down(n).start()
 
-    rs_first(NC - 1)
-    rs_second(NC - 2)
-    rs_third(NC - 3)
-    rs_last(NC - 4)
+    rs_1(6)
+    rs_2(5)
     step(1)
-    rs_second(NC - 1)
-    rs_third(NC - 2)
-    rs_last(NC - 3)
+    rs_2(6)
+    rs_3(4)
     step(2)
-    rs_third(NC - 1)
-    rs_last(NC - 2)
+    rs_3(5)
+    rs_4(0)
+    rs_4(1)
     step(3)
+    rs_3(6)
+    rs_4(2)
+    rs_4(3)
     mine = unit(z)
     go_up(3).wait_recv()
     go_down(3).wait_recv()
     last_s[...] = (mine + up_r[3].astype(F32) + dn_r[3].astype(F32)).astype(BF16)
     across = ring_copy(last_s.at[pl.ds(ho * 2, 2)], last_r, 8, to_h)
     across.start()
-    rs_last(NC - 1)
+    rs_4(4)
+    rs_4(5)
     across.wait_recv()
     for b in range(2):
         value = last_s[h * 2 + b].astype(F32) + last_r[b].astype(F32)
         dx_ref[:, b * B : (b + 1) * B] = value.T.astype(BF16)
 
+    rs_4(6)
+
     def sent(c, _):
-        for kind in range(1, 16):
+        for kind in (1, 2, 3, 4, 5, 7, 8, 9, 10, 11, 12, 13, 14, 15):
             ag(kind, 0, c, to_x, k).wait_send()
-        for kind in range(7):
+        for kind in range(1, 7):
             rs(kind, c, to_x).wait_send()
         rs_pair(c).wait_send()
+        either(c, sent_even, sent_odd)
         return 0
+
+    def sent_even(c):
+        ag(P2, 0, c, to_x, k).wait_send()
+        rs(0, c, to_x).wait_send()
+
+    def sent_odd(c):
+        ag_half(P2, 0, c, 0, to_yp).wait_send()
+        ag_half(HALF, 0, c, 1, to_ym).wait_send()
+        rs_half(c, 0).wait_send()
+        rs_half(c, 1).wait_send()
 
     lax.fori_loop(0, NC, sent, 0)
     for sem in range(15):
@@ -420,8 +523,8 @@
             dma((16, NC)),
             dma((15,)),
             dma((15,)),
-            dma((8, NC)),
-            dma((8, NC)),
+            dma((9, NC)),
+            dma((9, NC)),
             dma((9,)),
             dma((9,)),
         ],

time: 98.3 us -> 94.1 us (0.957)
  Pallas kernels: 91.5 us -> 86.5 us
    pallas_call x1, Pallas kernels: 91.5 us -> 86.5 us  [per_device(): pl.pallas_call(kernel, out_shape=(jax.ShapeDtypeStruct(grad_hidden.shape,...]
where the time goes in v2:
time: 94.1 us; the launch traced here: 92.6 us
  Pallas kernels  86.5 us (92%)
  local copies, waits for them, and re-layouts  5.41 us (6%)
    pallas_call x1, Pallas kernels, per_device(): pl.pallas_call(kernel, out_shape=(jax.ShapeDtypeStruct(grad_hidden.shape,...  86.5 us
    unnamed x11, local copies, waits for them, and re-layouts  5.41 us

profile of v2, /device:TPU:2, one launch (start us, length us, event | category | flops | bytes accessed | tf_op | source)
XLA Modules:
  0.0 92.6 jit_solution(13609973236504523076)
XLA Ops:
  0.6 1.4 %copy.9.mask_ref = s32[32,7]{1,0:T(8,128)} copy(s32[32,7]{0,1:T(8,128)} %param.8) | data formatting | bytes 1792 | tf_op args[3]
  2.0 86.5 %shard_map.84 = (bf16[128,896]{1,0:T(8,128)(2,1)}, bf16[128,256]{1,0:T(8,128)(2,1)}, bf16[1,7,128,128]{3,2,1,0:T(8,128)(2,1)}, bf16[1,7,128,128]{3,2,1,0:T(8,128)(2,1)}) custom-call(bf16[128,256]{1,0:T(8,128)(2,1)} %x_ref.1, bf16[1,7,128,128]{3,2,1,0:T(8,128)(2,1)} %g_ref.1, bf16[1,7,128,128]{3,2,1,0:T(8,128)(2,1)} %u_ref.1, s32[32,7]{1,0:T(8,128)} %copy.9.mask_ref, ...), custom_call_target="tpu_custom_call" | custom-call | flops 4000000000 | bytes 3145728 | tf_op jit(solution)/shard_map/pallas_call | solution.py:493
  88.6 0.0 copy-start.2
  88.6 0.0 copy-start.1
  88.6 1.7 %copy.14 = bf16[128,896]{1,0:T(8,128)(2,1)} copy(bf16[128,896]{1,0:T(8,128)(2,1)} %get-tuple-element.8) | data formatting | bytes 458752
  90.3 0.0 copy-done.2
  90.3 0.6 copy.15
  90.9 0.0 copy-done.1
  90.9 0.0 copy-start
  90.9 0.7 copy.16
  91.6 0.3 copy-done
  91.9 0.7 copy.17
Async XLA Ops:
  88.6 1.7 %copy-start.2 = (bf16[128,256]{1,0:T(8,128)(2,1)S(1)}, bf16[128,256]{1,0:T(8,128)(2,1)}, u32[]{:S(2)}) copy-start(bf16[128,256]{1,0:T(8,128)(2,1)} %get-tuple-element.9) | copy-start | bytes 196612
  88.6 2.3 %copy-start.1 = (bf16[1,7,128,128]{3,2,1,0:T(8,128)(2,1)S(1)}, bf16[1,7,128,128]{3,2,1,0:T(8,128)(2,1)}, u32[]{:S(2)}) copy-start(bf16[1,7,128,128]{3,2,1,0:T(8,128)(2,1)} %get-tuple-element.10) | copy-start | bytes 688132
  90.9 1.0 %copy-start = (bf16[1,7,128,128]{3,2,1,0:T(8,128)(2,1)S(1)}, bf16[1,7,128,128]{3,2,1,0:T(8,128)(2,1)}, u32[]{:S(2)}) copy-start(bf16[1,7,128,128]{3,2,1,0:T(8,128)(2,1)} %get-tuple-element.11) | copy-start | bytes 688132

commit v3 on v2

--- a/solution.py
+++ b/solution.py
@@ -59,7 +59,7 @@
         s = slot(*ring[which], core)
         return pltpu.make_async_remote_copy(
             src_ref=wbuf.at[s, c], dst_ref=wbuf.at[s, c],
-            send_sem=ag_s.at[kind, c], recv_sem=ag_r.at[kind, c],
+            send_sem=ag_s.at[c], recv_sem=ag_r.at[min(kind, 8), c],
             device_id=there, device_id_type=MESH,
         )
 
@@ -108,7 +108,7 @@
         s = slot(*ring[which], k)
         return pltpu.make_async_remote_copy(
             src_ref=wbuf.at[s, c, half], dst_ref=wbuf.at[s, c, half],
-            send_sem=ag_s.at[kind, c], recv_sem=ag_r.at[kind, c],
+            send_sem=ag_s.at[c], recv_sem=ag_r.at[kind, c],
             device_id=there, device_id_type=MESH,
         )
 
@@ -146,14 +146,17 @@
             pl.when(c % 2 == 1)(lambda: odd(c))
 
     def ag_end(c):
-        for which in range(8):
-            ag(8 + which, which, c, to_sib, ko).wait_recv()
+        pltpu.make_async_remote_copy(
+            src_ref=part_in.at[c], dst_ref=part_in.at[c],
+            send_sem=ag_s.at[c], recv_sem=ag_r.at[8, c],
+            device_id=to_sib, device_id_type=MESH,
+        ).wait_recv()
 
     def inp(sem, zz, hh, there):
         at = pl.ds(((zz + 8) % 8) * 4 + hh * 2, 2)
         return pltpu.make_async_remote_copy(
             src_ref=xbuf.at[at], dst_ref=xbuf.at[at],
-            send_sem=in_s.at[sem], recv_sem=in_r.at[sem],
+            send_sem=in_s.at[0], recv_sem=in_r.at[sem],
             device_id=there, device_id_type=MESH,
         )
 
@@ -232,14 +235,14 @@
     def rs(kind, c, there):
         return pltpu.make_async_remote_copy(
             src_ref=leave.at[kind, c], dst_ref=land.at[kind, c],
-            send_sem=rs_s.at[kind, c], recv_sem=rs_r.at[kind, c],
+            send_sem=rs_s.at[c], recv_sem=rs_r.at[kind, c],
             device_id=there, device_id_type=MESH,
         )
 
     def rs_pair(c):
         return pltpu.make_async_remote_copy(
             src_ref=part_out.at[c], dst_ref=part_in.at[c],
-            send_sem=rs_s.at[7, c], recv_sem=rs_r.at[7, c],
+            send_sem=rs_s.at[c], recv_sem=rs_r.at[7, c],
             device_id=to_sib, device_id_type=MESH,
         )
 
@@ -287,7 +290,7 @@
         there, sem = ((to_yp, 0), (to_ym, HALF_DN))[half]
         return pltpu.make_async_remote_copy(
             src_ref=leave.at[0, c, half], dst_ref=land.at[0, c, half],
-            send_sem=rs_s.at[sem, c], recv_sem=rs_r.at[sem, c],
+            send_sem=rs_s.at[c], recv_sem=rs_r.at[sem, c],
             device_id=there, device_id_type=MESH,
         )
 
@@ -394,41 +397,37 @@
 
     def ring_copy(src, dst, sem, there):
         return pltpu.make_async_remote_copy(
-            src_ref=src, dst_ref=dst, send_sem=dx_ss.at[sem], recv_sem=dx_rs.at[sem],
+            src_ref=src, dst_ref=dst, send_sem=dx_ss.at[0], recv_sem=dx_rs.at[sem],
             device_id=there, device_id_type=MESH,
         )
 
-    def go_up(n):
-        cut = pl.ds(0, 2 if n == 0 else 4)
-        return ring_copy(up_s.at[n, cut], up_r.at[n, cut], n, to_zp)
-
-    def go_down(n):
-        cut = pl.ds(2, 2) if n == 0 else pl.ds(0, 4)
-        return ring_copy(dn_s.at[n, cut], dn_r.at[n, cut], 4 + n, to_zm)
+    def go_up(n, half):
+        cut = pl.ds(2 * half, 2)
+        return ring_copy(up_s.at[n, cut], up_r.at[n, cut], 2 * n + half, to_zp)
+
+    def go_down(n, half):
+        cut = pl.ds(2 * half, 2)
+        return ring_copy(dn_s.at[n, cut], dn_r.at[n, cut], 8 + 2 * n + half, to_zm)
 
     far = unit((z + 4) % 8).astype(BF16)
     up_s[0, :2] = far[:2]
-    go_up(0).start()
+    go_up(0, 0).start()
     dn_s[0, 2:] = far[2:]
-    go_down(0).start()
+    go_down(0, 1).start()
+
+    def pass_on(n, go, out, came, mine, order):
+        for half in order:
+            cut = slice(2 * half, 2 * half + 2)
+            value = mine[cut]
+            if n > 1 or half == order[1]:
+                go(n - 1, half).wait_recv()
+                value = value + came[n - 1, cut].astype(F32)
+            out[n, cut] = value.astype(BF16)
+            go(n, half).start()
 
     def step(n):
-        mine = unit((z + 4 - n) % 8)
-        go_up(n - 1).wait_recv()
-        if n == 1:
-            up_s[n, :2] = (mine[:2] + up_r[0, :2].astype(F32)).astype(BF16)
-            up_s[n, 2:] = mine[2:].astype(BF16)
-        else:
-            up_s[n] = (mine + up_r[n - 1].astype(F32)).astype(BF16)
-        go_up(n).start()
-        mine = unit((z + 4 + n) % 8)
-        go_down(n - 1).wait_recv()
-        if n == 1:
-            dn_s[n, :2] = mine[:2].astype(BF16)
-            dn_s[n, 2:] = (mine[2:] + dn_r[0, 2:].astype(F32)).astype(BF16)
-        else:
-            dn_s[n] = (mine + dn_r[n - 1].astype(F32)).astype(BF16)
-        go_down(n).start()
+        pass_on(n, go_up, up_s, up_r, unit((z + 4 - n) % 8), (1, 0))
+        pass_on(n, go_down, dn_s, dn_r, unit((z + 4 + n) % 8), (0, 1))
 
     rs_1(6)
     rs_2(5)
@@ -444,10 +443,11 @@
     rs_4(2)
     rs_4(3)
     mine = unit(z)
-    go_up(3).wait_recv()
-    go_down(3).wait_recv()
+    for half in range(2):
+        go_up(3, half).wait_recv()
+        go_down(3, half).wait_recv()
     last_s[...] = (mine + up_r[3].astype(F32) + dn_r[3].astype(F32)).astype(BF16)
-    across = ring_copy(last_s.at[pl.ds(ho * 2, 2)], last_r, 8, to_h)
+    across = ring_copy(last_s.at[pl.ds(ho * 2, 2)], last_r, 16, to_h)
     across.start()
     rs_4(4)
     rs_4(5)
@@ -458,32 +458,21 @@
 
     rs_4(6)
 
-    def sent(c, _):
-        for kind in (1, 2, 3, 4, 5, 7, 8, 9, 10, 11, 12, 13, 14, 15):
-            ag(kind, 0, c, to_x, k).wait_send()
-        for kind in range(1, 7):
-            rs(kind, c, to_x).wait_send()
-        rs_pair(c).wait_send()
-        either(c, sent_even, sent_odd)
+    def sent(sem):
+        pltpu.make_async_remote_copy(
+            src_ref=xbuf.at[pl.ds(0, 30)], dst_ref=xbuf.at[pl.ds(0, 30)],
+            send_sem=sem, recv_sem=in_r.at[0],
+            device_id=to_h, device_id_type=MESH,
+        ).wait_send()
+
+    def column_sent(c, _):
+        sent(ag_s.at[c])
+        sent(rs_s.at[c])
         return 0
 
-    def sent_even(c):
-        ag(P2, 0, c, to_x, k).wait_send()
-        rs(0, c, to_x).wait_send()
-
-    def sent_odd(c):
-        ag_half(P2, 0, c, 0, to_yp).wait_send()
-        ag_half(HALF, 0, c, 1, to_ym).wait_send()
-        rs_half(c, 0).wait_send()
-        rs_half(c, 1).wait_send()
-
-    lax.fori_loop(0, NC, sent, 0)
-    for sem in range(15):
-        inp(sem, z, h, to_h).wait_send()
-    for n in range(4):
-        go_up(n).wait_send()
-        go_down(n).wait_send()
-    across.wait_send()
+    lax.fori_loop(0, NC, column_sent, 0)
+    sent(in_s.at[0])
+    sent(dx_ss.at[0])
 
 
 def per_device(inputs, gate_blocks, up_blocks, block_mask, grad_hidden):
@@ -519,14 +508,14 @@
             pltpu.SMEM((RB, NC), jnp.int32),
             pltpu.SMEM((KEEP, NC), jnp.int32),
             pltpu.SMEM((RB,), jnp.int32),
-            dma((16, NC)),
-            dma((16, NC)),
+            dma((NC,)),
+            dma((9, NC)),
+            dma((1,)),
             dma((15,)),
-            dma((15,)),
+            dma((NC,)),
             dma((9, NC)),
-            dma((9, NC)),
-            dma((9,)),
-            dma((9,)),
+            dma((1,)),
+            dma((17,)),
         ],
         compiler_params=pltpu.CompilerParams(
             collective_id=0, has_side_effects=True, vmem_limit_bytes=56 * 2**20

time: 94.1 us -> 90.2 us (0.959)
  Pallas kernels: 86.5 us -> 82.8 us
    pallas_call x1, Pallas kernels: 86.5 us -> 82.8 us  [per_device(): pl.pallas_call(kernel, out_shape=(jax.ShapeDtypeStruct(grad_hidden.shape,...]
where the time goes in v3:
time: 90.2 us; the launch traced here: 88.9 us
  Pallas kernels  82.8 us (92%)
  local copies, waits for them, and re-layouts  5.41 us (6%)
    pallas_call x1, Pallas kernels, per_device(): pl.pallas_call(kernel, out_shape=(jax.ShapeDtypeStruct(grad_hidden.shape,...  82.8 us
    unnamed x11, local copies, waits for them, and re-layouts  5.41 us

profile of v3, /device:TPU:2, one launch (start us, length us, event | category | flops | bytes accessed | tf_op | source)
XLA Modules:
  0.0 88.9 jit_solution(6981584568358393000)
XLA Ops:
  0.6 1.4 %copy.9.mask_ref = s32[32,7]{1,0:T(8,128)} copy(s32[32,7]{0,1:T(8,128)} %param.8) | data formatting | bytes 1792 | tf_op args[3]
  2.0 82.8 %shard_map.84 = (bf16[128,896]{1,0:T(8,128)(2,1)}, bf16[128,256]{1,0:T(8,128)(2,1)}, bf16[1,7,128,128]{3,2,1,0:T(8,128)(2,1)}, bf16[1,7,128,128]{3,2,1,0:T(8,128)(2,1)}) custom-call(bf16[128,256]{1,0:T(8,128)(2,1)} %x_ref.1, bf16[1,7,128,128]{3,2,1,0:T(8,128)(2,1)} %g_ref.1, bf16[1,7,128,128]{3,2,1,0:T(8,128)(2,1)} %u_ref.1, s32[32,7]{1,0:T(8,128)} %copy.9.mask_ref, ...), custom_call_target="tpu_custom_call" | custom-call | flops 4000000000 | bytes 3145728 | tf_op jit(solution)/shard_map/pallas_call | solution.py:482
  84.8 0.0 copy-start.2
  84.9 0.0 copy-start.1
  84.9 1.7 %copy.14 = bf16[128,896]{1,0:T(8,128)(2,1)} copy(bf16[128,896]{1,0:T(8,128)(2,1)} %get-tuple-element.8) | data formatting | bytes 458752
  86.6 0.0 copy-done.2
  86.6 0.6 copy.15
  87.2 0.0 copy-done.1
  87.2 0.0 copy-start
  87.2 0.7 copy.16
  87.9 0.3 copy-done
  88.2 0.7 copy.17
Async XLA Ops:
  84.8 1.7 %copy-start.2 = (bf16[128,256]{1,0:T(8,128)(2,1)S(1)}, bf16[128,256]{1,0:T(8,128)(2,1)}, u32[]{:S(2)}) copy-start(bf16[128,256]{1,0:T(8,128)(2,1)} %get-tuple-element.9) | copy-start | bytes 196612
  84.9 2.3 %copy-start.1 = (bf16[1,7,128,128]{3,2,1,0:T(8,128)(2,1)S(1)}, bf16[1,7,128,128]{3,2,1,0:T(8,128)(2,1)}, u32[]{:S(2)}) copy-start(bf16[1,7,128,128]{3,2,1,0:T(8,128)(2,1)} %get-tuple-element.10) | copy-start | bytes 688132
  87.2 1.0 %copy-start = (bf16[1,7,128,128]{3,2,1,0:T(8,128)(2,1)S(1)}, bf16[1,7,128,128]{3,2,1,0:T(8,128)(2,1)}, u32[]{:S(2)}) copy-start(bf16[1,7,128,128]{3,2,1,0:T(8,128)(2,1)} %get-tuple-element.11) | copy-start | bytes 688132

commit v4 on v3

--- a/solution.py
+++ b/solution.py
@@ -376,13 +376,9 @@
         def _():
             rs_1(c - 1)
 
-        @pl.when(c >= 2)
-        def _():
-            rs_2(c - 2)
-
         @pl.when(c >= 3)
         def _():
-            rs_3(c - 3)
+            rs_2(c - 3)
 
         return 0
 
@@ -430,18 +426,20 @@
         pass_on(n, go_down, dn_s, dn_r, unit((z + 4 + n) % 8), (0, 1))
 
     rs_1(6)
+    rs_2(4)
     rs_2(5)
     step(1)
+    rs_3(0)
+    rs_3(1)
+    rs_3(2)
     rs_2(6)
+    step(2)
+    rs_3(3)
     rs_3(4)
-    step(2)
+    rs_4(0)
+    step(3)
     rs_3(5)
-    rs_4(0)
     rs_4(1)
-    step(3)
-    rs_3(6)
-    rs_4(2)
-    rs_4(3)
     mine = unit(z)
     for half in range(2):
         go_up(3, half).wait_recv()
@@ -449,6 +447,9 @@
     last_s[...] = (mine + up_r[3].astype(F32) + dn_r[3].astype(F32)).astype(BF16)
     across = ring_copy(last_s.at[pl.ds(ho * 2, 2)], last_r, 16, to_h)
     across.start()
+    rs_3(6)
+    rs_4(2)
+    rs_4(3)
     rs_4(4)
     rs_4(5)
     across.wait_recv()

time: 90.2 us -> 82.1 us (0.910); the launches traced: 88.9 us -> 81.9 us
  Pallas kernels: 82.8 us -> 75.8 us
    pallas_call x1, Pallas kernels: 82.8 us -> 75.8 us  [per_device(): pl.pallas_call(kernel, out_shape=(jax.ShapeDtypeStruct(grad_hidden.shape,...]
where the time goes in v4:
time: 82.1 us; the launch traced here: 81.9 us
  Pallas kernels  75.8 us (92%)
  local copies, waits for them, and re-layouts  5.41 us (7%)
    pallas_call x1, Pallas kernels, per_device(): pl.pallas_call(kernel, out_shape=(jax.ShapeDtypeStruct(grad_hidden.shape,...  75.8 us
    unnamed x11, local copies, waits for them, and re-layouts  5.41 us

profile of v4, /device:TPU:2, one launch (start us, length us, event | category | flops | bytes accessed | tf_op | source)
XLA Modules:
  0.0 81.9 jit_solution(6521820270057483708)
XLA Ops:
  0.6 1.4 %copy.9.mask_ref = s32[32,7]{1,0:T(8,128)} copy(s32[32,7]{0,1:T(8,128)} %param.8) | data formatting | bytes 1792 | tf_op args[3]
  2.0 75.8 %shard_map.84 = (bf16[128,896]{1,0:T(8,128)(2,1)}, bf16[128,256]{1,0:T(8,128)(2,1)}, bf16[1,7,128,128]{3,2,1,0:T(8,128)(2,1)}, bf16[1,7,128,128]{3,2,1,0:T(8,128)(2,1)}) custom-call(bf16[128,256]{1,0:T(8,128)(2,1)} %x_ref.1, bf16[1,7,128,128]{3,2,1,0:T(8,128)(2,1)} %g_ref.1, bf16[1,7,128,128]{3,2,1,0:T(8,128)(2,1)} %u_ref.1, s32[32,7]{1,0:T(8,128)} %copy.9.mask_ref, ...), custom_call_target="tpu_custom_call" | custom-call | flops 4000000000 | bytes 3145728 | tf_op jit(solution)/shard_map/pallas_call | solution.py:483
  77.9 0.0 copy-start.2
  77.9 0.0 copy-start.1
  77.9 1.7 %copy.14 = bf16[128,896]{1,0:T(8,128)(2,1)} copy(bf16[128,896]{1,0:T(8,128)(2,1)} %get-tuple-element.8) | data formatting | bytes 458752
  79.6 0.0 copy-done.2
  79.6 0.6 copy.15
  80.2 0.0 copy-done.1
  80.2 0.0 copy-start
  80.2 0.7 copy.16
  80.9 0.3 copy-done
  81.2 0.7 copy.17
Async XLA Ops:
  77.9 1.7 %copy-start.2 = (bf16[128,256]{1,0:T(8,128)(2,1)S(1)}, bf16[128,256]{1,0:T(8,128)(2,1)}, u32[]{:S(2)}) copy-start(bf16[128,256]{1,0:T(8,128)(2,1)} %get-tuple-element.9) | copy-start | bytes 196612
  77.9 2.3 %copy-start.1 = (bf16[1,7,128,128]{3,2,1,0:T(8,128)(2,1)S(1)}, bf16[1,7,128,128]{3,2,1,0:T(8,128)(2,1)}, u32[]{:S(2)}) copy-start(bf16[1,7,128,128]{3,2,1,0:T(8,128)(2,1)} %get-tuple-element.10) | copy-start | bytes 688132
  80.2 1.0 %copy-start = (bf16[1,7,128,128]{3,2,1,0:T(8,128)(2,1)S(1)}, bf16[1,7,128,128]{3,2,1,0:T(8,128)(2,1)}, u32[]{:S(2)}) copy-start(bf16[1,7,128,128]{3,2,1,0:T(8,128)(2,1)} %get-tuple-element.11) | copy-start | bytes 688132

commit v5 on v4

--- a/solution.py
+++ b/solution.py
@@ -427,19 +427,17 @@
 
     rs_1(6)
     rs_2(4)
+    step(1)
     rs_2(5)
-    step(1)
     rs_3(0)
     rs_3(1)
-    rs_3(2)
     rs_2(6)
     step(2)
+    rs_3(2)
     rs_3(3)
+    step(3)
     rs_3(4)
-    rs_4(0)
-    step(3)
     rs_3(5)
-    rs_4(1)
     mine = unit(z)
     for half in range(2):
         go_up(3, half).wait_recv()
@@ -448,6 +446,8 @@
     across = ring_copy(last_s.at[pl.ds(ho * 2, 2)], last_r, 16, to_h)
     across.start()
     rs_3(6)
+    rs_4(0)
+    rs_4(1)
     rs_4(2)
     rs_4(3)
     rs_4(4)

time: 82.1 us -> 79.7 us (0.971)
  Pallas kernels: 75.8 us -> 73.5 us
    pallas_call x1, Pallas kernels: 75.8 us -> 73.5 us  [per_device(): pl.pallas_call(kernel, out_shape=(jax.ShapeDtypeStruct(grad_hidden.shape,...]
where the time goes in v5:
time: 79.7 us; the launch traced here: 79.5 us
  Pallas kernels  73.5 us (92%)
  local copies, waits for them, and re-layouts  5.41 us (7%)
    pallas_call x1, Pallas kernels, per_device(): pl.pallas_call(kernel, out_shape=(jax.ShapeDtypeStruct(grad_hidden.shape,...  73.5 us
    unnamed x11, local copies, waits for them, and re-layouts  5.41 us

profile of v5, /device:TPU:2, one launch (start us, length us, event | category | flops | bytes accessed | tf_op | source)
XLA Modules:
  0.0 79.5 jit_solution(4691205712411176186)
XLA Ops:
  0.6 1.4 %copy.9.mask_ref = s32[32,7]{1,0:T(8,128)} copy(s32[32,7]{0,1:T(8,128)} %param.8) | data formatting | bytes 1792 | tf_op args[3]
  2.0 73.5 %shard_map.84 = (bf16[128,896]{1,0:T(8,128)(2,1)}, bf16[128,256]{1,0:T(8,128)(2,1)}, bf16[1,7,128,128]{3,2,1,0:T(8,128)(2,1)}, bf16[1,7,128,128]{3,2,1,0:T(8,128)(2,1)}) custom-call(bf16[128,256]{1,0:T(8,128)(2,1)} %x_ref.1, bf16[1,7,128,128]{3,2,1,0:T(8,128)(2,1)} %g_ref.1, bf16[1,7,128,128]{3,2,1,0:T(8,128)(2,1)} %u_ref.1, s32[32,7]{1,0:T(8,128)} %copy.9.mask_ref, ...), custom_call_target="tpu_custom_call" | custom-call | flops 4000000000 | bytes 3145728 | tf_op jit(solution)/shard_map/pallas_call | solution.py:483
  75.5 0.0 copy-start.2
  75.5 0.0 copy-start.1
  75.5 1.7 %copy.14 = bf16[128,896]{1,0:T(8,128)(2,1)} copy(bf16[128,896]{1,0:T(8,128)(2,1)} %get-tuple-element.8) | data formatting | bytes 458752
  77.2 0.0 copy-done.2
  77.2 0.6 copy.15
  77.8 0.0 copy-done.1
  77.8 0.0 copy-start
  77.8 0.7 copy.16
  78.5 0.3 copy-done
  78.8 0.7 copy.17
Async XLA Ops:
  75.5 1.7 %copy-start.2 = (bf16[128,256]{1,0:T(8,128)(2,1)S(1)}, bf16[128,256]{1,0:T(8,128)(2,1)}, u32[]{:S(2)}) copy-start(bf16[128,256]{1,0:T(8,128)(2,1)} %get-tuple-element.9) | copy-start | bytes 196612
  75.5 2.3 %copy-start.1 = (bf16[1,7,128,128]{3,2,1,0:T(8,128)(2,1)S(1)}, bf16[1,7,128,128]{3,2,1,0:T(8,128)(2,1)}, u32[]{:S(2)}) copy-start(bf16[1,7,128,128]{3,2,1,0:T(8,128)(2,1)} %get-tuple-element.10) | copy-start | bytes 688132
  77.8 1.0 %copy-start = (bf16[1,7,128,128]{3,2,1,0:T(8,128)(2,1)S(1)}, bf16[1,7,128,128]{3,2,1,0:T(8,128)(2,1)}, u32[]{:S(2)}) copy-start(bf16[1,7,128,128]{3,2,1,0:T(8,128)(2,1)} %get-tuple-element.11) | copy-start | bytes 688132
